TPU v7x, 32 devices: a whole 2x2x4 slice. The times are simulated.
32 devices in a mesh: runs: 2 (over x), tm: 8 (over z, y), hyd: 2 (over core).
Axes of the slice: x: 2, y: 2, z: 4, core: 2. Of those that a mesh axis runs over, the one named last changes fastest.
Arguments:
- record: bfloat16 [524160, 1024], P(('runs', 'tm'), 'hyd'), parts along dimension 0, may hold values from -6 to 6
- chips: int32 [4095], replicated, may hold values from -1 to 1, as said below
- steer_lags: int32 [1024, 256], P('hyd'), may hold values from 0 to 7
Outputs:
- power: float32 [128, 512, 256], P('runs', 'tm', 'hyd'), parts along dimension 0
There are 2 independent parts, one for each index of `runs`. A program takes and returns all parts, laid end to end along the dimension named above; an argument that names none is the same for every part. Nothing has to cross between parts.
Inputs may be any that keep to these rules, and one draw needn't show every extreme that they name: The chips are +1 or -1 and form one period of a maximal-length sequence of period 4095, starting at a drawn phase.
All inputs are finite; a program needn't handle non-finite values.
Results may differ from a plain program's by a relative error of at most 0.0047.
Values may be sent and summed in bfloat16 or wider, within the bound.
A program may use at most 256 MiB of HBM per device.

v0:
```python
import math
import jax
import jax.numpy as jnp
from jax import lax
from jax.sharding import PartitionSpec as P

CODE = 4095
HYDRO = 1024
DELAYS = 512
PERIODS = 64
BEAMS = 256
MAXLAG = 8


def passed_along(array, axis, by):
    length = lax.axis_size(axis)
    pairs = [(i, i + by) for i in range(length) if 0 <= i + by < length]
    return lax.ppermute(array, axis, pairs)


def toeplitz_code(chips):
    seg_len = CODE + DELAYS - 1
    padded = jnp.concatenate([chips.astype(jnp.float32), jnp.zeros((DELAYS,), jnp.float32)])
    tiled = jnp.tile(padded, DELAYS)[: DELAYS * seg_len]
    return tiled.reshape(DELAYS, seg_len).astype(jnp.bfloat16)


def dft_table(length):
    freq = jnp.arange(length, dtype=jnp.int32)
    phase = (freq[:, None] * freq[None, :] % length).astype(jnp.float32) * (2.0 * math.pi / length)
    weight = 1.0 / math.sqrt(length)
    return jnp.concatenate([jnp.cos(phase) * weight, -jnp.sin(phase) * weight], 0).astype(
        jnp.bfloat16
    )


def body(record, chips, steer_lags):
    hyd_local = record.shape[1]
    tm_size = lax.axis_size("tm")
    local_periods = PERIODS // tm_size
    delay_rows = DELAYS // tm_size
    seg_len = CODE + DELAYS - 1
    norm_code = 1.0 / math.sqrt(CODE)
    tail_rows = passed_along(record[: DELAYS - 1], "tm", -1)
    extended = jnp.concatenate([record, tail_rows], 0)
    toeplitz = toeplitz_code(chips)
    profile_list = []
    for period in range(local_periods):
        segment = extended[period * CODE : period * CODE + seg_len]
        profile_list.append(
            (jnp.dot(toeplitz, segment, preferred_element_type=jnp.float32) * norm_code).astype(
                jnp.bfloat16
            )
        )
    profiles = jnp.stack(profile_list, 0)
    transform = dft_table(PERIODS)
    received = lax.all_to_all(profiles, "tm", split_axis=1, concat_axis=0, tiled=True)
    trailing = received.shape[1:]
    flattened = received.reshape(received.shape[0], -1)
    spectral = jnp.dot(transform, flattened, preferred_element_type=jnp.float32).astype(
        jnp.bfloat16
    )
    spectrum = spectral.reshape((2, received.shape[0]) + trailing)
    next_rows = passed_along(spectrum[:, :, : MAXLAG - 1, :], "tm", -1)
    spec_ext = jnp.concatenate([spectrum, next_rows], 2)
    norm_hydro = 1.0 / math.sqrt(HYDRO)
    shifted_list = [
        spec_ext[:, :, offset : offset + delay_rows, :].reshape(2 * PERIODS * delay_rows, hyd_local)
        for offset in range(MAXLAG)
    ]
    beam_local = BEAMS // lax.axis_size("hyd")
    partial_sum = jnp.zeros((2 * PERIODS * delay_rows, BEAMS), jnp.float32)
    for offset in range(MAXLAG):
        selector = (steer_lags == offset).astype(jnp.bfloat16)
        partial_sum = partial_sum + jnp.dot(
            shifted_list[offset], selector, preferred_element_type=jnp.float32
        )
    summed = lax.psum(partial_sum * norm_hydro, "hyd")
    owned = lax.dynamic_slice_in_dim(summed, lax.axis_index("hyd") * beam_local, beam_local, 1)
    owned = owned.reshape(2, PERIODS, delay_rows, beam_local)
    return owned[0] * owned[0] + owned[1] * owned[1]


def solution(mesh):
    in_specs = (P(("runs", "tm"), "hyd"), P(), P("hyd", None))
    out_specs = P("runs", "tm", "hyd")
    return jax.shard_map(body, mesh=mesh, in_specs=in_specs, out_specs=out_specs, check_vma=False)
```

profile of v0, /device:TPU:0, one launch (start us, length us, event | category | flops | bytes accessed | tf_op | source)
XLA Modules:
  0.0 408.6 jit_solution(9783359401931948476)
XLA Ops:
  6.5 1.1 slice.73
  7.6 1.3 collective-permute-start
  8.9 0.7 convert_element_type.49
  9.6 2.5 tile.10
  12.1 11.8 %tile.11 = bf16[2358784]{0:T(1024)(128)(2,1)} reshape(bf16[512,4607]{1,0:T(8,128)(2,1)} %tile.10) | data formatting | bytes 9435136 | tf_op jit(solution)/shard_map/tile | solution.py:24
  23.9 5.7 %slice.85 = bf16[2358272]{0:T(1024)(128)(2,1)} slice(bf16[2358784]{0:T(1024)(128)(2,1)} %tile.11), slice={[0:2358272]} | slice | bytes 9433088 | tf_op jit(solution)/shard_map/slice | solution.py:24
  29.6 11.3 %convert_element_type.50 = bf16[512,4606]{1,0:T(8,128)(2,1)} reshape(bf16[2358272]{0:T(1024)(128)(2,1)} %slice.85) | data formatting | bytes 9433088 | tf_op jit(solution)/shard_map/convert_element_type | solution.py:25
  40.9 7.3 %fusion.65 = bf16[8,512,512]{2,1,0:T(8,128)(2,1)} fusion(bf16[512,4606]{1,0:T(8,128)(2,1)} %convert_element_type.50, bf16[32760,512]{1,0:T(8,128)(2,1)} %param.3), kind=kOutput, calls=%fused_computation.47 | convolution fusion | flops 2415394816 | bytes 9961472 | tf_op jit(solution)/shard_map/dot_general | solution.py:51
  48.2 0.0 copy-done.1
  48.2 0.0 slice-start.2
  48.2 0.0 slice-start.3
  48.2 0.0 slice-start.4
  48.3 0.0 slice-start.5
  48.3 0.0 slice-start.6
  48.3 5.9 %fusion.73 = bf16[8,512,512]{2,1,0:T(8,128)(2,1)} fusion(bf16[8,512,512]{2,1,0:T(8,128)(2,1)} %fusion.65, bf16[512,4606]{1,0:T(8,128)(2,1)S(1)} %copy-done.1, bf16[32760,512]{1,0:T(8,128)(2,1)} %param.3), kind=kOutput, calls=%fused_computation.51 | convolution fusion | flops 2415394816 | bytes 9959424 | tf_op jit(solution)/shard_map/dot_general | solution.py:51
  54.2 0.0 slice-start.7
  54.2 6.6 %fusion.79 = bf16[8,512,512]{2,1,0:T(8,128)(2,1)} fusion(bf16[8,512,512]{2,1,0:T(8,128)(2,1)} %fusion.73, bf16[512,4606]{1,0:T(8,128)(2,1)S(1)} %copy-done.1, bf16[32760,512]{1,0:T(8,128)(2,1)} %param.3), kind=kOutput, calls=%fused_computation.53 | convolution fusion | flops 2415394816 | bytes 9959424 | tf_op jit(solution)/shard_map/dot_general | solution.py:51
  60.8 0.0 slice-done.2
  60.8 0.0 slice-done.3
  60.8 0.0 slice-done.4
  60.8 0.0 slice-done.5
  60.8 0.0 slice-done.6
  60.9 0.0 slice-done.7
  60.9 0.0 slice-done.8
  60.9 1.4 slice-done.9
  62.3 3.7 fusion.85
  66.0 3.5 fusion.91
  69.5 3.5 fusion.97
  73.0 3.5 fusion.103
  76.5 0.0 collective-permute-done
  76.5 5.9 %fusion.69 = bf16[8,512,512]{2,1,0:T(8,128)(2,1)} fusion(bf16[8,512,512]{2,1,0:T(8,128)(2,1)} %fusion.103, bf16[512,4606]{1,0:T(8,128)(2,1)} %convert_element_type.50, bf16[511,512]{1,0:T(8,128)(2,1)S(1)} %collective-permute-done, bf16[32760,512]{1,0:T(8,128)(2,1)S(1)} %bitcast.82), kind=kOutput, calls=%fused_computation.49 | convolution fusion | flops 2424827904 | bytes 39312384 | tf_op jit(solution)/shard_map/dot_general | solution.py:51
  82.5 6.9 %copy.5 = bf16[8,512,512]{2,0,1:T(8,128)(2,1)} copy(bf16[8,512,512]{2,1,0:T(8,128)(2,1)} %fusion.69) | data formatting | bytes 8388608 | tf_op jit(solution)/shard_map/stack | solution.py:55
  89.3 8.4 %all-to-all-start = ((bf16[8,512,512]{2,0,1:T(8,128)(2,1)}), bf16[8,512,512]{2,0,1:T(8,128)(2,1)}, u32[]{:S(2)}, u32[]{:S(2)}) async-start(bf16[8,512,512]{2,0,1:T(8,128)(2,1)} %copy.5), calls=%async_computation | async-start | bytes 8388608 | tf_op jit(solution)/shard_map/all_to_all | solution.py:57
  97.8 0.0 all-reduce.3.cloned.1.call-start
  97.8 0.2 multiply_convert_fusion
  98.0 92.8 %all-to-all-done = bf16[8,512,512]{2,0,1:T(8,128)(2,1)} async-done(((bf16[8,512,512]{2,0,1:T(8,128)(2,1)}), bf16[8,512,512]{2,0,1:T(8,128)(2,1)}, u32[]{:S(2)}, u32[]{:S(2)}) %all-to-all-start) | async-done | bytes 4194336 | tf_op jit(solution)/shard_map/all_to_all | solution.py:57
  190.8 3.8 copy.14
  194.6 2.6 copy.10
  197.1 5.6 %convolution_convert_fusion = bf16[128,32768]{1,0:T(8,128)(2,1)} fusion(bf16[64,32768]{1,0:T(8,128)(2,1)S(1)} %bitcast.83, bf16[64,64]{1,0:T(8,128)(2,1)S(1)} %get-tuple-element.12, bf16[64,64]{1,0:T(8,128)(2,1)S(1)} %get-tuple-element.13), kind=kOutput, calls=%fused_computation | convolution fusion | flops 541097984 | bytes 12599296 | tf_op jit(solution)/shard_map/dot_general | solution.py:60
  202.7 13.6 %reshape_reshape.3 = bf16[8192,512]{1,0:T(8,128)(2,1)} reshape(bf16[128,32768]{1,0:T(8,128)(2,1)} %convolution_convert_fusion) | data formatting | bytes 16777216 | tf_op jit(solution)/shard_map/reshape;reshape | solution.py:68
  216.3 10.2 %copy.11 = bf16[16,8,64,512]{3,2,1,0:T(8,128)(2,1)} copy(bf16[16,8,64,512]{3,1,2,0:T(8,128)(2,1)} %bitcast.69) | data formatting | bytes 16777216
  226.6 8.0 %constant_dynamic-update-slice_fusion = bf16[2,64,71,512]{3,2,1,0:T(8,128)(2,1)} fusion(bf16[2,64,64,512]{3,2,1,0:T(8,128)(2,1)} %bitcast.79), kind=kLoop, calls=%fused_computation.94 | loop fusion | bytes 16777216
  234.6 1.3 slice.86
  235.9 0.3 copy.9
  236.2 1.3 collective-permute-start.1
  237.5 0.0 copy-done
  237.5 9.1 %fusion.113 = f32[8192,256]{1,0:T(8,128)} fusion(bf16[8192,512]{1,0:T(8,128)(2,1)} %reshape_reshape.3, s32[512,256]{1,0:T(8,128)S(1)} %copy-done), kind=kOutput, calls=%fused_computation.70 | convolution fusion | flops 2147614720 | bytes 17301504 | tf_op jit(solution)/shard_map/dot_general | solution.py:75
  246.7 12.5 %collective-permute-done.1 = bf16[2,64,7,512]{3,1,2,0:T(8,128)(2,1)S(1)} collective-permute-done((bf16[2,64,7,512]{3,1,2,0:T(8,128)(2,1)S(1)}, bf16[2,64,7,512]{3,1,2,0:T(8,128)(2,1)S(1)}, u32[]{:S(2)}, u32[]{:S(2)}) %collective-permute-start.1) | collective-permute-done | bytes 917536 | tf_op jit(solution)/shard_map/ppermute | solution.py:18
  259.1 1.6 copy_dynamic-update-slice_fusion
  260.7 52.8 %fusion.142 = (bf16[2,64,64,512]{3,2,1,0:T(8,128)(2,1)}, bf16[2,64,64,512]{3,2,1,0:T(8,128)(2,1)}, bf16[2,64,64,512]{3,2,1,0:T(8,128)(2,1)}, bf16[2,64,64,512]{3...) fusion(bf16[2,64,71,512]{3,2,1,0:T(8,128)(2,1)} %copy_dynamic-u, ...), kind=kLoop, calls=%fused_computation.106 | loop fusion | bytes 117440512 | tf_op jit(solution)/shard_map/slice | solution.py:68
  313.6 8.4 %convolution_add_fusion.6 = f32[8192,256]{1,0:T(8,128)S(1)} fusion(f32[8192,256]{1,0:T(8,128)} %fusion.113, bf16[8192,512]{1,0:T(8,128)(2,1)} %bitcast.78, s32[512,256]{1,0:T(8,128)S(1)} %copy-done), kind=kOutput, calls=%fused_computation.8 | convolution fusion | flops 2149711872 | bytes 25690112 | tf_op jit(solution)/shard_map/dot_general | solution.py:75
  322.0 0.0 slice-start
  322.0 6.1 %convolution_add_fusion.5 = f32[8192,256]{1,0:T(8,128)S(1)} fusion(f32[8192,256]{1,0:T(8,128)S(1)} %convolution_add_fusion.6, bf16[8192,512]{1,0:T(8,128)(2,1)} %bitcast.77, s32[512,256]{1,0:T(8,128)S(1)} %copy-done), kind=kOutput, calls=%fused_computation.7 | convolution fusion | flops 2149711872 | bytes 25690112 | tf_op jit(solution)/shard_map/dot_general | solution.py:75
  328.1 0.0 slice-start.1
  328.1 6.1 %convolution_add_fusion.4 = f32[8192,256]{1,0:T(8,128)S(1)} fusion(f32[8192,256]{1,0:T(8,128)S(1)} %convolution_add_fusion.5, bf16[8192,512]{1,0:T(8,128)(2,1)} %bitcast.76, s32[512,256]{1,0:T(8,128)S(1)} %copy-done), kind=kOutput, calls=%fused_computation.6 | convolution fusion | flops 2149711872 | bytes 25690112 | tf_op jit(solution)/shard_map/dot_general | solution.py:75
  334.3 0.0 slice-done
  334.3 0.0 slice-done.1
  334.3 2.4 convolution_add_fusion.3
  336.7 6.3 %convolution_add_fusion.2 = f32[8192,256]{1,0:T(8,128)S(1)} fusion(f32[8192,256]{1,0:T(8,128)S(1)} %convolution_add_fusion.3, bf16[8192,512]{1,0:T(8,128)(2,1)} %bitcast.72, s32[512,256]{1,0:T(8,128)S(1)} %copy-done), kind=kOutput, calls=%fused_computation.4 | convolution fusion | flops 2149711872 | bytes 25690112 | tf_op jit(solution)/shard_map/dot_general | solution.py:75
  343.0 6.0 %convolution_add_fusion.1 = f32[8192,256]{1,0:T(8,128)S(1)} fusion(f32[8192,256]{1,0:T(8,128)S(1)} %convolution_add_fusion.2, bf16[8192,512]{1,0:T(8,128)(2,1)} %bitcast.71, s32[512,256]{1,0:T(8,128)S(1)} %copy-done), kind=kOutput, calls=%fused_computation.3 | convolution fusion | flops 2149711872 | bytes 25690112 | tf_op jit(solution)/shard_map/dot_general | solution.py:75
  349.0 9.2 %fusion = f32[8192,256]{1,0:T(8,128)} fusion(f32[8192,256]{1,0:T(8,128)S(1)} %convolution_add_fusion.1, bf16[8192,512]{1,0:T(8,128)(2,1)} %bitcast.70, s32[512,256]{1,0:T(8,128)S(1)} %copy-done), kind=kOutput, calls=%fused_computation.2 | convolution fusion | flops 2151809024 | bytes 25690112 | tf_op jit(solution)/shard_map/dot_general | solution.py:75
  358.2 0.0 all-reduce.3.cloned.1.call-update
  358.2 39.2 %all-reduce.3.cloned.1.call-done = f32[8192,256]{1,0:T(8,128)} async-done(((f32[8192,256]{1,0:T(8,128)}), f32[8192,256]{1,0:T(8,128)}) %all-reduce.3.cloned.1.call-update) | async-done | bytes 8388624 | tf_op jit(solution)/shard_map/psum | solution.py:78
  397.5 3.8 fusion.17
  (7 shorter events, 0.0 us)
Async XLA Ops:
  7.6 68.9 %collective-permute-start = (bf16[511,512]{1,0:T(8,128)(2,1)S(1)}, bf16[511,512]{1,0:T(8,128)(2,1)S(1)}, u32[]{:S(2)}, u32[]{:S(2)}) collective-permute-start(bf16[511,512]{1,0:T(8,128)(2,1)S(1)} %slice.73), channel_id=1, source_target_pairs={{2,0},{4,2},{6,4},{8,6},{10,8},{12,10},{14,12},{3,1},{5,3},{7,5},{... | collective-permute-start | bytes 1569800 | tf_op jit(solution)/shard_map/ppermute | solution.py:18
  40.9 7.3 %copy-start.1 = (bf16[512,4606]{1,0:T(8,128)(2,1)S(1)}, bf16[512,4606]{1,0:T(8,128)(2,1)}, u32[]{:S(2)}) copy-start(bf16[512,4606]{1,0:T(8,128)(2,1)} %convert_element_type.50) | copy-start | bytes 14149636
  48.2 12.6 %slice-start.2 = ((s8[33546240]{0:T(1024)(128)(4,1)}), s8[4194304]{0:T(1024)(128)(4,1)S(1)}, s32[]{:S(2)}) async-start(s8[33546240]{0:T(1024)(128)(4,1)} %bitcast.81), calls=%async_computation.4 | async-start | bytes 8388608
  48.2 12.6 %slice-start.3 = ((s8[33546240]{0:T(1024)(128)(4,1)}), s8[4194304]{0:T(1024)(128)(4,1)S(1)}, s32[]{:S(2)}) async-start(s8[33546240]{0:T(1024)(128)(4,1)} %bitcast.81), calls=%async_computation.5 | async-start | bytes 8388608
  48.2 12.6 %slice-start.4 = ((s8[33546240]{0:T(1024)(128)(4,1)}), s8[4194304]{0:T(1024)(128)(4,1)S(1)}, s32[]{:S(2)}) async-start(s8[33546240]{0:T(1024)(128)(4,1)} %bitcast.81), calls=%async_computation.6 | async-start | bytes 8388608
  48.3 12.6 %slice-start.5 = ((s8[33546240]{0:T(1024)(128)(4,1)}), s8[4194304]{0:T(1024)(128)(4,1)S(1)}, s32[]{:S(2)}) async-start(s8[33546240]{0:T(1024)(128)(4,1)} %bitcast.81), calls=%async_computation.7 | async-start | bytes 8388608
  48.3 12.6 %slice-start.6 = ((s8[33546240]{0:T(1024)(128)(4,1)}), s8[4194304]{0:T(1024)(128)(4,1)S(1)}, s32[]{:S(2)}) async-start(s8[33546240]{0:T(1024)(128)(4,1)} %bitcast.81), calls=%async_computation.8 | async-start | bytes 8388608
  54.2 6.6 %slice-start.7 = ((s8[33546240]{0:T(1024)(128)(4,1)}), s8[4194304]{0:T(1024)(128)(4,1)S(1)}, s32[]{:S(2)}) async-start(s8[33546240]{0:T(1024)(128)(4,1)} %bitcast.81), calls=%async_computation.9 | async-start | bytes 8388608
  54.2 6.7 %slice-start.8 = ((s8[33546240]{0:T(1024)(128)(4,1)}), s8[4194304]{0:T(1024)(128)(4,1)S(1)}, s32[]{:S(2)}) async-start(s8[33546240]{0:T(1024)(128)(4,1)} %bitcast.81), calls=%async_computation.10 | async-start | bytes 8388608
  54.2 8.0 %slice-start.9 = ((s8[33546240]{0:T(1024)(128)(4,1)}), s8[4186112]{0:T(1024)(128)(4,1)S(1)}, s32[]{:S(2)}) async-start(s8[33546240]{0:T(1024)(128)(4,1)} %bitcast.81), calls=%async_computation.11 | async-start | bytes 8372224
  89.3 101.4 %all-to-all-start = ((bf16[8,512,512]{2,0,1:T(8,128)(2,1)}), bf16[8,512,512]{2,0,1:T(8,128)(2,1)}, u32[]{:S(2)}, u32[]{:S(2)}) async-start(bf16[8,512,512]{2,0,1:T(8,128)(2,1)} %copy.5), calls=%async_computation | async-start | bytes 8388608 | tf_op jit(solution)/shard_map/all_to_all | solution.py:57
  97.8 299.7 %all-reduce.3.cloned.1.call-start = ((), (), s32[]{:S(2)}) async-start(), calls=%async_computation.1 | async-start | bytes 16777216 | tf_op jit(solution)/shard_map/psum | solution.py:78
  226.6 10.9 %copy-start = (s32[512,256]{1,0:T(8,128)S(1)}, s32[512,256]{1,0:T(8,128)}, u32[]{:S(2)}) copy-start(s32[512,256]{1,0:T(8,128)} %param.5) | copy-start | bytes 1572868
  236.2 22.9 %collective-permute-start.1 = (bf16[2,64,7,512]{3,1,2,0:T(8,128)(2,1)S(1)}, bf16[2,64,7,512]{3,1,2,0:T(8,128)(2,1)S(1)}, u32[]{:S(2)}, u32[]{:S(2)}) collective-permute-start(bf16[2,64,7,512]{3,1,2,0:T(8,128)(2,1)S(1)} %copy.9), channel_id=1, source_target_pairs={{2,0},{4,2},{6,4},{8,6},{10,8},{12,10},{14,12},{3,1},{5,3},{7,5},{... | collective-permute-start | bytes 2752520 | tf_op jit(solution)/shard_map/ppermute | solution.py:18
  322.0 12.3 %slice-start = ((s8[8388608]{0:T(1024)(128)(4,1)}), s8[4194304]{0:T(1024)(128)(4,1)S(1)}, s32[]{:S(2)}) async-start(s8[8388608]{0:T(1024)(128)(4,1)} %bitcast.73), calls=%async_computation.2 | async-start | bytes 8388608
  328.1 6.2 %slice-start.1 = ((s8[8388608]{0:T(1024)(128)(4,1)}), s8[4194304]{0:T(1024)(128)(4,1)S(1)}, s32[]{:S(2)}) async-start(s8[8388608]{0:T(1024)(128)(4,1)} %bitcast.73), calls=%async_computation.3 | async-start | bytes 8388608
Sparse Core Ops, SparseCore 0:
  358.3 39.0 all-reduce.2
where the time goes:
time: 416 us; the launch traced here: 409 us
  waiting for transfers between devices  145 us (35%)
  local copies, waits for them, and re-layouts  135 us (32%)
  matrix products  99.3 us (24%)
  between operations  14.1 us (3%)
  starting transfers between devices  11 us (3%)
  other arithmetic  4.64 us (1%)
    all_to_all x1, waiting for transfers between devices, body(): lax.all_to_all(profiles, 'tm', split_axis=1, concat_axis=0, tiled=True)  92.8 us
    dot_general x8, matrix products, body(): jnp.dot(shifted_list[offset], selector, preferred_element_type=jnp.float32)  53.7 us
    slice x1, local copies, waits for them, and re-layouts, body(): spec_ext[:, :, offset:offset + delay_rows, :]  52.8 us
    dot_general x8, matrix products, body(): jnp.dot(toeplitz, segment, preferred_element_type=jnp.float32) * norm_code  40 us
    psum x1, waiting for transfers between devices, body(): summed = lax.psum(partial_sum * norm_hydro, 'hyd')  39.2 us
    unnamed x28, local copies, waits for them, and re-layouts  22.6 us
    another operation x2, local copies, waits for them, and re-layouts, toeplitz_code(): tiled = jnp.tile(padded, DELAYS)[:DELAYS * seg_len]  14.3 us
    another operation x1, local copies, waits for them, and re-layouts, body(): spec_ext[:, :, offset:offset + delay_rows, :]  13.6 us
  transfers between devices with their start and end apart: 4, of which 3 were waited for; matrix products, arithmetic and copies ran while one was open for 18% of the time, Pallas kernels for 0%

commit v1 on v0

--- a/solution.py
+++ b/solution.py
@@ -54,7 +54,10 @@
         )
     profiles = jnp.stack(profile_list, 0)
     transform = dft_table(PERIODS)
-    received = lax.all_to_all(profiles, "tm", split_axis=1, concat_axis=0, tiled=True)
+    received = jnp.concatenate(
+        lax.all_to_all(jnp.stack(jnp.split(profiles, lax.axis_size("tm"), axis=1)), "tm", 0, 0),
+        axis=0,
+    )
     trailing = received.shape[1:]
     flattened = received.reshape(received.shape[0], -1)
     spectral = jnp.dot(transform, flattened, preferred_element_type=jnp.float32).astype(

time: 416 us -> 415 us (level)
  matrix products: 99.3 us -> 92 us
  local copies, waits for them, and re-layouts: 135 us -> 142 us
    unnamed x28 -> x43, local copies, waits for them, and re-layouts: 22.6 us -> 37.8 us
    dot_general x8, matrix products: 53.7 us -> 46.4 us  [body(): jnp.dot(shifted_list[offset], selector, preferred_element_type=jnp.float32)]
    another operation x2, local copies, waits for them, and re-layouts: 6.88 us -> 1.92 us  [the longest x1 1.91 us: body(): jnp.stack(jnp.split(profiles, lax.axis_size('tm'), axis=1))]
  transfers between devices with their start and end apart: 4 -> 4, of which waited for: 3 -> 3; matrix products, arithmetic and copies ran while one was open for 18% -> 19% of each run, Pallas kernels for 0% -> 0%
where the time goes in v1:
time: 415 us; the launch traced here: 408 us
  waiting for transfers between devices  144 us (35%)
  local copies, waits for them, and re-layouts  142 us (34%)
  matrix products  92 us (22%)
  between operations  13.9 us (3%)
  starting transfers between devices  11.7 us (3%)
  other arithmetic  4.64 us (1%)
    all_to_all x1, waiting for transfers between devices, body(): lax.all_to_all(jnp.stack(jnp.split(profiles, lax.axis_size('tm'), axis=1)...  92.6 us
    slice x1, local copies, waits for them, and re-layouts, body(): spec_ext[:, :, offset:offset + delay_rows, :]  53 us
    dot_general x8, matrix products, body(): jnp.dot(shifted_list[offset], selector, preferred_element_type=jnp.float32)  46.4 us
    dot_general x8, matrix products, body(): jnp.dot(toeplitz, segment, preferred_element_type=jnp.float32) * norm_code  39.9 us
    psum x1, waiting for transfers between devices, body(): summed = lax.psum(partial_sum * norm_hydro, 'hyd')  39.2 us
    unnamed x43, local copies, waits for them, and re-layouts  37.8 us
    another operation x2, local copies, waits for them, and re-layouts, toeplitz_code(): tiled = jnp.tile(padded, DELAYS)[:DELAYS * seg_len]  14.3 us
    another operation x1, local copies, waits for them, and re-layouts, body(): spec_ext[:, :, offset:offset + delay_rows, :]  13.5 us
  transfers between devices with their start and end apart: 4, of which 3 were waited for; matrix products, arithmetic and copies ran while one was open for 19% of the time, Pallas kernels for 0%

profile of v1, /device:TPU:0, one launch (start us, length us, event | category | flops | bytes accessed | tf_op | source)
XLA Modules:
  0.0 407.7 jit_solution(14679334907386854929)
XLA Ops:
  6.5 1.1 slice.73
  7.6 1.3 collective-permute-start
  8.9 0.7 convert_element_type.49
  9.6 2.5 tile.10
  12.1 11.8 %tile.11 = bf16[2358784]{0:T(1024)(128)(2,1)} reshape(bf16[512,4607]{1,0:T(8,128)(2,1)} %tile.10) | data formatting | bytes 9435136 | tf_op jit(solution)/shard_map/tile | solution.py:24
  23.9 5.9 %slice.85 = bf16[2358272]{0:T(1024)(128)(2,1)} slice(bf16[2358784]{0:T(1024)(128)(2,1)} %tile.11), slice={[0:2358272]} | slice | bytes 9433088 | tf_op jit(solution)/shard_map/slice | solution.py:24
  29.8 11.3 %convert_element_type.50 = bf16[512,4606]{1,0:T(8,128)(2,1)} reshape(bf16[2358272]{0:T(1024)(128)(2,1)} %slice.85) | data formatting | bytes 9433088 | tf_op jit(solution)/shard_map/convert_element_type | solution.py:25
  41.2 7.3 %fusion.65 = bf16[8,512,512]{2,1,0:T(8,128)(2,1)} fusion(bf16[512,4606]{1,0:T(8,128)(2,1)} %convert_element_type.50, bf16[32760,512]{1,0:T(8,128)(2,1)} %param.3), kind=kOutput, calls=%fused_computation.46 | convolution fusion | flops 2415394816 | bytes 9961472 | tf_op jit(solution)/shard_map/dot_general | solution.py:51
  48.5 0.0 slice-start.9
  48.5 0.0 slice-start.10
  48.5 5.9 %fusion.73 = bf16[8,512,512]{2,1,0:T(8,128)(2,1)} fusion(bf16[8,512,512]{2,1,0:T(8,128)(2,1)} %fusion.65, bf16[512,4606]{1,0:T(8,128)(2,1)S(1)} %copy-done.1, bf16[32760,512]{1,0:T(8,128)(2,1)} %param.3), kind=kOutput, calls=%fused_computation.50 | convolution fusion | flops 2415394816 | bytes 9959424 | tf_op jit(solution)/shard_map/dot_general | solution.py:51
  54.5 6.6 %fusion.79 = bf16[8,512,512]{2,1,0:T(8,128)(2,1)} fusion(bf16[8,512,512]{2,1,0:T(8,128)(2,1)} %fusion.73, bf16[512,4606]{1,0:T(8,128)(2,1)S(1)} %copy-done.1, bf16[32760,512]{1,0:T(8,128)(2,1)} %param.3), kind=kOutput, calls=%fused_computation.52 | convolution fusion | flops 2415394816 | bytes 9959424 | tf_op jit(solution)/shard_map/dot_general | solution.py:51
  61.1 0.0 slice-done.9
  61.1 0.0 slice-done.10
  61.1 0.0 slice-done.11
  61.1 0.1 slice-done.12
  61.1 1.4 slice-done.13
  62.5 3.7 fusion.85
  66.2 3.5 fusion.91
  69.7 3.5 fusion.97
  73.2 3.5 fusion.103
  76.7 0.0 collective-permute-done
  76.7 5.9 %fusion.69 = bf16[8,512,512]{2,1,0:T(8,128)(2,1)} fusion(bf16[8,512,512]{2,1,0:T(8,128)(2,1)} %fusion.103, bf16[512,4606]{1,0:T(8,128)(2,1)} %convert_element_type.50, bf16[511,512]{1,0:T(8,128)(2,1)S(1)} %collective-permute-done, bf16[32760,512]{1,0:T(8,128)(2,1)S(1)} %bitcast.114), kind=kOutput, calls=%fused_computation.48 | convolution fusion | flops 2424827904 | bytes 39312384 | tf_op jit(solution)/shard_map/dot_general | solution.py:51
  82.6 1.9 fusion.113
  84.5 1.9 fusion.112
  86.3 1.9 fusion.111
  88.2 1.9 fusion.110
  90.1 1.9 fusion.109
  91.9 1.9 fusion.108
  93.8 1.9 fusion.107
  95.7 1.9 fusion.106
  97.6 8.4 %all-to-all-start = ((bf16[8,8,64,512]{3,2,1,0:T(8,128)(2,1)}), bf16[8,8,64,512]{3,2,1,0:T(8,128)(2,1)}, u32[]{:S(2)}, u32[]{:S(2)}) async-start(bf16[8,8,64,512]{3,2,1,0:T(8,128)(2,1)} %fusion.106), calls=%async_computation | async-start | bytes 8388608 | tf_op jit(solution)/shard_map/all_to_all | solution.py:58
  106.0 0.2 all-reduce.3.cloned.1.call-start
  106.3 0.2 multiply_convert_fusion
  106.4 92.6 %all-to-all-done = bf16[8,8,64,512]{3,2,1,0:T(8,128)(2,1)} async-done(((bf16[8,8,64,512]{3,2,1,0:T(8,128)(2,1)}), bf16[8,8,64,512]{3,2,1,0:T(8,128)(2,1)}, u32[]{:S(2)}, u32[]{:S(2)}) %all-to-all-start) | async-done | bytes 4194336 | tf_op jit(solution)/shard_map/all_to_all | solution.py:58
  199.0 4.7 %copy.7 = bf16[8,8,64,512]{3,1,2,0:T(8,128)(2,1)S(1)} copy(bf16[8,8,64,512]{3,2,1,0:T(8,128)(2,1)} %all-to-all-done) | data formatting | bytes 8388608
  203.8 5.6 %convolution_convert_fusion = bf16[128,32768]{1,0:T(8,128)(2,1)} fusion(bf16[64,32768]{1,0:T(8,128)(2,1)S(1)} %bitcast.115, bf16[64,64]{1,0:T(8,128)(2,1)S(1)} %get-tuple-element.12, bf16[64,64]{1,0:T(8,128)(2,1)S(1)} %get-tuple-element.13), kind=kOutput, calls=%fused_computation | convolution fusion | flops 541097984 | bytes 12599296 | tf_op jit(solution)/shard_map/dot_general | solution.py:63
  209.4 13.5 %reshape_reshape.7 = bf16[8192,512]{1,0:T(8,128)(2,1)} reshape(bf16[128,32768]{1,0:T(8,128)(2,1)} %convolution_convert_fusion) | data formatting | bytes 16777216 | tf_op jit(solution)/shard_map/reshape;reshape | solution.py:71
  222.8 10.2 %copy.8 = bf16[16,8,64,512]{3,2,1,0:T(8,128)(2,1)} copy(bf16[16,8,64,512]{3,1,2,0:T(8,128)(2,1)} %bitcast.97) | data formatting | bytes 16777216
  233.1 8.0 %constant_dynamic-update-slice_fusion = bf16[2,64,71,512]{3,2,1,0:T(8,128)(2,1)} fusion(bf16[2,64,64,512]{3,2,1,0:T(8,128)(2,1)} %bitcast.111), kind=kLoop, calls=%fused_computation.98 | loop fusion | bytes 16777216
  241.0 1.3 slice.86
  242.3 0.3 copy.6
  242.6 1.7 collective-permute-start.1
  244.3 0.0 copy-done
  244.4 9.1 %fusion.121 = f32[8192,256]{1,0:T(8,128)} fusion(bf16[8192,512]{1,0:T(8,128)(2,1)} %reshape_reshape.7, s32[512,256]{1,0:T(8,128)S(1)} %copy-done), kind=kOutput, calls=%fused_computation.85 | convolution fusion | flops 2147614720 | bytes 17301504 | tf_op jit(solution)/shard_map/dot_general | solution.py:78
  253.5 12.1 %collective-permute-done.1 = bf16[2,64,7,512]{3,1,2,0:T(8,128)(2,1)S(1)} collective-permute-done((bf16[2,64,7,512]{3,1,2,0:T(8,128)(2,1)S(1)}, bf16[2,64,7,512]{3,1,2,0:T(8,128)(2,1)S(1)}, u32[]{:S(2)}, u32[]{:S(2)}) %collective-permute-start.1) | collective-permute-done | bytes 917536 | tf_op jit(solution)/shard_map/ppermute | solution.py:18
  265.6 1.5 copy_dynamic-update-slice_fusion
  267.1 53.0 %fusion.150 = (bf16[2,64,64,512]{3,2,1,0:T(8,128)(2,1)}, bf16[2,64,64,512]{3,2,1,0:T(8,128)(2,1)}, bf16[2,64,64,512]{3,2,1,0:T(8,128)(2,1)}, bf16[2,64,64,512]{3...) fusion(bf16[2,64,71,512]{3,2,1,0:T(8,128)(2,1)} %copy_dynamic-u, ...), kind=kLoop, calls=%fused_computation.121 | loop fusion | bytes 117440512 | tf_op jit(solution)/shard_map/slice | solution.py:71
  320.1 0.0 slice-start.4
  320.1 0.0 slice-start.5
  320.1 8.4 %convolution_add_fusion.6 = f32[8192,256]{1,0:T(8,128)S(1)} fusion(f32[8192,256]{1,0:T(8,128)} %fusion.121, bf16[8192,512]{1,0:T(8,128)(2,1)} %bitcast.110, s32[512,256]{1,0:T(8,128)S(1)} %copy-done), kind=kOutput, calls=%fused_computation.8 | convolution fusion | flops 2149711872 | bytes 25690112 | tf_op jit(solution)/shard_map/dot_general | solution.py:78
  328.6 2.4 convolution_add_fusion.5
  331.0 0.0 slice-start.2
  331.0 0.0 slice-start.3
  331.0 6.1 %convolution_add_fusion.4 = f32[8192,256]{1,0:T(8,128)S(1)} fusion(f32[8192,256]{1,0:T(8,128)S(1)} %convolution_add_fusion.5, bf16[8192,512]{1,0:T(8,128)(2,1)} %bitcast.106, s32[512,256]{1,0:T(8,128)S(1)} %copy-done), kind=kOutput, calls=%fused_computation.6 | convolution fusion | flops 2149711872 | bytes 25690112 | tf_op jit(solution)/shard_map/dot_general | solution.py:78
  337.2 2.4 convolution_add_fusion.3
  339.6 6.2 %convolution_add_fusion.2 = f32[8192,256]{1,0:T(8,128)S(1)} fusion(f32[8192,256]{1,0:T(8,128)S(1)} %convolution_add_fusion.3, bf16[8192,512]{1,0:T(8,128)(2,1)} %bitcast.102, s32[512,256]{1,0:T(8,128)S(1)} %copy-done), kind=kOutput, calls=%fused_computation.4 | convolution fusion | flops 2149711872 | bytes 25690112 | tf_op jit(solution)/shard_map/dot_general | solution.py:78
  345.8 0.0 slice-start
  345.8 0.0 slice-start.1
  345.8 6.1 %convolution_add_fusion.1 = f32[8192,256]{1,0:T(8,128)S(1)} fusion(f32[8192,256]{1,0:T(8,128)S(1)} %convolution_add_fusion.2, bf16[8192,512]{1,0:T(8,128)(2,1)} %bitcast.101, s32[512,256]{1,0:T(8,128)S(1)} %copy-done), kind=kOutput, calls=%fused_computation.3 | convolution fusion | flops 2149711872 | bytes 25690112 | tf_op jit(solution)/shard_map/dot_general | solution.py:78
  352.0 5.7 %fusion = f32[8192,256]{1,0:T(8,128)} fusion(f32[8192,256]{1,0:T(8,128)S(1)} %convolution_add_fusion.1, bf16[8192,512]{1,0:T(8,128)(2,1)S(1)} %bitcast.100, s32[512,256]{1,0:T(8,128)S(1)} %copy-done), kind=kOutput, calls=%fused_computation.2 | convolution fusion | flops 2151809024 | bytes 25690112 | tf_op jit(solution)/shard_map/dot_general | solution.py:78
  357.6 0.0 all-reduce.3.cloned.1.call-update
  357.7 39.2 %all-reduce.3.cloned.1.call-done = f32[8192,256]{1,0:T(8,128)} async-done(((f32[8192,256]{1,0:T(8,128)}), f32[8192,256]{1,0:T(8,128)}) %all-reduce.3.cloned.1.call-update) | async-done | bytes 8388624 | tf_op jit(solution)/shard_map/psum | solution.py:81
  396.9 3.8 fusion.17
  (23 shorter events, 0.0 us)
Async XLA Ops:
  7.6 69.1 %collective-permute-start = (bf16[511,512]{1,0:T(8,128)(2,1)S(1)}, bf16[511,512]{1,0:T(8,128)(2,1)S(1)}, u32[]{:S(2)}, u32[]{:S(2)}) collective-permute-start(bf16[511,512]{1,0:T(8,128)(2,1)S(1)} %slice.73), channel_id=1, source_target_pairs={{2,0},{4,2},{6,4},{8,6},{10,8},{12,10},{14,12},{3,1},{5,3},{7,5},{... | collective-permute-start | bytes 1569800 | tf_op jit(solution)/shard_map/ppermute | solution.py:18
  41.2 7.3 %copy-start.1 = (bf16[512,4606]{1,0:T(8,128)(2,1)S(1)}, bf16[512,4606]{1,0:T(8,128)(2,1)}, u32[]{:S(2)}) copy-start(bf16[512,4606]{1,0:T(8,128)(2,1)} %convert_element_type.50) | copy-start | bytes 14149636
  48.5 12.6 %slice-start.6 = ((s8[33546240]{0:T(1024)(128)(4,1)}), s8[4194304]{0:T(1024)(128)(4,1)S(1)}, s32[]{:S(2)}) async-start(s8[33546240]{0:T(1024)(128)(4,1)} %bitcast.113), calls=%async_computation.8 | async-start | bytes 8388608
  48.5 12.6 %slice-start.7 = ((s8[33546240]{0:T(1024)(128)(4,1)}), s8[4194304]{0:T(1024)(128)(4,1)S(1)}, s32[]{:S(2)}) async-start(s8[33546240]{0:T(1024)(128)(4,1)} %bitcast.113), calls=%async_computation.9 | async-start | bytes 8388608
  48.5 12.6 %slice-start.8 = ((s8[33546240]{0:T(1024)(128)(4,1)}), s8[4194304]{0:T(1024)(128)(4,1)S(1)}, s32[]{:S(2)}) async-start(s8[33546240]{0:T(1024)(128)(4,1)} %bitcast.113), calls=%async_computation.10 | async-start | bytes 8388608
  48.5 12.6 %slice-start.9 = ((s8[33546240]{0:T(1024)(128)(4,1)}), s8[4194304]{0:T(1024)(128)(4,1)S(1)}, s32[]{:S(2)}) async-start(s8[33546240]{0:T(1024)(128)(4,1)} %bitcast.113), calls=%async_computation.11 | async-start | bytes 8388608
  48.5 12.6 %slice-start.10 = ((s8[33546240]{0:T(1024)(128)(4,1)}), s8[4194304]{0:T(1024)(128)(4,1)S(1)}, s32[]{:S(2)}) async-start(s8[33546240]{0:T(1024)(128)(4,1)} %bitcast.113), calls=%async_computation.12 | async-start | bytes 8388608
  54.5 6.6 %slice-start.11 = ((s8[33546240]{0:T(1024)(128)(4,1)}), s8[4194304]{0:T(1024)(128)(4,1)S(1)}, s32[]{:S(2)}) async-start(s8[33546240]{0:T(1024)(128)(4,1)} %bitcast.113), calls=%async_computation.13 | async-start | bytes 8388608
  54.5 6.7 %slice-start.12 = ((s8[33546240]{0:T(1024)(128)(4,1)}), s8[4194304]{0:T(1024)(128)(4,1)S(1)}, s32[]{:S(2)}) async-start(s8[33546240]{0:T(1024)(128)(4,1)} %bitcast.113), calls=%async_computation.14 | async-start | bytes 8388608
  54.5 8.1 %slice-start.13 = ((s8[33546240]{0:T(1024)(128)(4,1)}), s8[4186112]{0:T(1024)(128)(4,1)S(1)}, s32[]{:S(2)}) async-start(s8[33546240]{0:T(1024)(128)(4,1)} %bitcast.113), calls=%async_computation.15 | async-start | bytes 8372224
  97.6 101.4 %all-to-all-start = ((bf16[8,8,64,512]{3,2,1,0:T(8,128)(2,1)}), bf16[8,8,64,512]{3,2,1,0:T(8,128)(2,1)}, u32[]{:S(2)}, u32[]{:S(2)}) async-start(bf16[8,8,64,512]{3,2,1,0:T(8,128)(2,1)} %fusion.106), calls=%async_computation | async-start | bytes 8388608 | tf_op jit(solution)/shard_map/all_to_all | solution.py:58
  106.0 290.9 %all-reduce.3.cloned.1.call-start = ((), (), s32[]{:S(2)}) async-start(), calls=%async_computation.1 | async-start | bytes 16777216 | tf_op jit(solution)/shard_map/psum | solution.py:81
  233.1 11.3 %copy-start = (s32[512,256]{1,0:T(8,128)S(1)}, s32[512,256]{1,0:T(8,128)}, u32[]{:S(2)}) copy-start(s32[512,256]{1,0:T(8,128)} %param.5) | copy-start | bytes 1572868
  242.6 22.9 %collective-permute-start.1 = (bf16[2,64,7,512]{3,1,2,0:T(8,128)(2,1)S(1)}, bf16[2,64,7,512]{3,1,2,0:T(8,128)(2,1)S(1)}, u32[]{:S(2)}, u32[]{:S(2)}) collective-permute-start(bf16[2,64,7,512]{3,1,2,0:T(8,128)(2,1)S(1)} %copy.6), channel_id=1, source_target_pairs={{2,0},{4,2},{6,4},{8,6},{10,8},{12,10},{14,12},{3,1},{5,3},{7,5},{... | collective-permute-start | bytes 2752520 | tf_op jit(solution)/shard_map/ppermute | solution.py:18
  320.1 8.4 %slice-start.4 = ((s8[8388608]{0:T(1024)(128)(4,1)}), s8[4194304]{0:T(1024)(128)(4,1)S(1)}, s32[]{:S(2)}) async-start(s8[8388608]{0:T(1024)(128)(4,1)} %bitcast.107), calls=%async_computation.6 | async-start | bytes 8388608
  320.1 8.4 %slice-start.5 = ((s8[8388608]{0:T(1024)(128)(4,1)}), s8[4194304]{0:T(1024)(128)(4,1)S(1)}, s32[]{:S(2)}) async-start(s8[8388608]{0:T(1024)(128)(4,1)} %bitcast.107), calls=%async_computation.7 | async-start | bytes 8388608
  331.0 6.2 %slice-start.2 = ((s8[8388608]{0:T(1024)(128)(4,1)}), s8[4194304]{0:T(1024)(128)(4,1)S(1)}, s32[]{:S(2)}) async-start(s8[8388608]{0:T(1024)(128)(4,1)} %bitcast.103), calls=%async_computation.4 | async-start | bytes 8388608
  331.0 6.2 %slice-start.3 = ((s8[8388608]{0:T(1024)(128)(4,1)}), s8[4194304]{0:T(1024)(128)(4,1)S(1)}, s32[]{:S(2)}) async-start(s8[8388608]{0:T(1024)(128)(4,1)} %bitcast.103), calls=%async_computation.5 | async-start | bytes 8388608
  345.8 6.2 %slice-start = ((s8[8388608]{0:T(1024)(128)(4,1)}), s8[4194304]{0:T(1024)(128)(4,1)S(1)}, s32[]{:S(2)}) async-start(s8[8388608]{0:T(1024)(128)(4,1)} %bitcast.98), calls=%async_computation.2 | async-start | bytes 8388608
  345.8 6.2 %slice-start.1 = ((s8[8388608]{0:T(1024)(128)(4,1)}), s8[4194304]{0:T(1024)(128)(4,1)S(1)}, s32[]{:S(2)}) async-start(s8[8388608]{0:T(1024)(128)(4,1)} %bitcast.98), calls=%async_computation.3 | async-start | bytes 8388608
Sparse Core Ops, SparseCore 0:
  357.8 39.0 all-reduce.2
